TPU v7x, 256 devices: a whole 4x4x8 slice. The times are simulated.
256 devices in a mesh: seq: 64 (over y, z, core), chan: 4 (over x).
Axes of the slice: x: 4, y: 4, z: 8, core: 2. Of those that a mesh axis runs over, the one named last changes fastest.
Arguments:
- inputs: bfloat16 [32768, 1536], P('seq', 'chan'), may hold values from -16 to 16
- conv_weight: bfloat16 [1, 3, 1536, 1536], P(None, None, None, 'chan'), may hold values from -0.09375 to 0.09375
- head_weight: bfloat16 [1536, 4096], P(None, 'chan'), may hold values from -0.15625 to 0.15625
- head_cot: bfloat16 [32768, 4096], P('seq', 'chan'), may hold values from -6 to 6
- exon_blocks: int32 [512, 8], P('seq'), may hold values from 0 to 255
Outputs:
- tracks: bfloat16 [32768, 4096], P('seq', 'chan')
- coverage: float32 [512, 4096], P('seq', 'chan')
- input_grad: bfloat16 [32768, 1536], P('seq', 'chan')
- kernel_gradient: float32 [1, 3, 1536, 1536], P(None, None, 'seq', 'chan')
All inputs are finite; a program needn't handle non-finite values.
Results may differ from a plain program's by a relative error of at most 0.0059.
Values may be sent and summed in bfloat16 or wider, within the bound.
No kernel may reach another device: no remote copies, remote signals or barrier semaphores. Data moves between devices by JAX's collectives and lax.ppermute only.
A program may use at most 64 MiB of HBM per device.

v0:
```python
import jax
import jax.numpy as jnp
from jax import lax
from jax.sharding import PartitionSpec as P

BLOCK = 128
EXONS = 8


def shifted(value, axis, steps):
    count = lax.axis_size(axis)
    leading, last = (max(0, -steps), min(count, count - steps))
    return lax.ppermute(value, axis, [(source, source + steps) for source in range(leading, last)])


def activation_slope(point, cotan):
    _, back = jax.vjp(jax.nn.gelu, point)
    return back(cotan)[0]


def tap_input(values, steps):
    return shifted(values, "seq", steps)


def tap_grad(values, steps):
    return shifted(values, "seq", steps)


def times_t(left, right):
    return lax.dot_general(
        left, right, (((1,), (1,)), ((), ())), preferred_element_type=jnp.float32
    )


def inner_rows(left, right):
    return lax.dot_general(
        left, right, (((0,), (0,)), ((), ())), preferred_element_type=jnp.float32
    )


def shards(inputs, conv_weight, head_weight, head_cot, exon_blocks):
    rows = inputs.shape[0]
    state = inputs
    layer_number = 0
    steps = 2 * 2**layer_number
    acted = jax.nn.gelu(state.astype(jnp.float32)).astype(jnp.bfloat16)
    lower = tap_input(acted, steps)
    upper = tap_input(acted, -steps)
    whole = lax.all_gather(acted, "chan", axis=1, tiled=True)
    whole_low = lax.all_gather(lower, "chan", axis=1, tiled=True)
    whole_up = lax.all_gather(upper, "chan", axis=1, tiled=True)
    mixed = jnp.dot(whole_low, conv_weight[layer_number, 0], preferred_element_type=jnp.float32)
    mixed = mixed + jnp.dot(whole, conv_weight[layer_number, 1], preferred_element_type=jnp.float32)
    mixed = mixed + jnp.dot(
        whole_up, conv_weight[layer_number, 2], preferred_element_type=jnp.float32
    )
    saved = [(state, whole, steps)]
    state = (state.astype(jnp.float32) + mixed).astype(jnp.bfloat16)
    full_state = lax.all_gather(state, "chan", axis=1, tiled=True)
    logits = jnp.dot(full_state, head_weight, preferred_element_type=jnp.float32)
    tracks = jax.nn.softplus(logits).astype(jnp.bfloat16)
    head_term = (head_cot.astype(jnp.float32) * jax.nn.sigmoid(logits)).astype(jnp.bfloat16)
    grad = lax.psum_scatter(
        times_t(head_term, head_weight), "chan", scatter_dimension=1, tiled=True
    )
    grads = []
    for layer_number in reversed(range(conv_weight.shape[0])):
        before, whole, steps = saved[layer_number]
        grad_low = grad.astype(jnp.bfloat16)
        later = tap_grad(grad_low, -steps)
        earlier = tap_grad(grad_low, steps)
        partial_value = times_t(later, conv_weight[layer_number, 0])
        partial_value = partial_value + times_t(grad_low, conv_weight[layer_number, 1])
        partial_value = partial_value + times_t(earlier, conv_weight[layer_number, 2])
        back_u = lax.psum_scatter(partial_value, "chan", scatter_dimension=1, tiled=True)
        kernel = jnp.stack(
            [inner_rows(whole, later), inner_rows(whole, grad_low), inner_rows(whole, earlier)]
        )
        grads.append(lax.psum_scatter(kernel, "seq", scatter_dimension=1, tiled=True))
        grad = grad + activation_slope(before.astype(jnp.float32), back_u)
    kernel_gradient = jnp.stack(grads[::-1])
    resident_blocks = rows // BLOCK
    block_partial_sums = (
        tracks.astype(jnp.float32).reshape(resident_blocks, BLOCK, tracks.shape[1]).sum(axis=1)
    )
    scale = jnp.sqrt(jnp.float32(EXONS * BLOCK))
    all_blocks = lax.all_gather(block_partial_sums, "seq", axis=0, tiled=True)
    labels = jnp.arange(all_blocks.shape[0], dtype=jnp.int32)
    counts = jnp.sum((exon_blocks[:, :, None] == labels[None, None, :]).astype(jnp.float32), axis=1)
    coverage = jnp.dot(counts, all_blocks, precision=lax.Precision.HIGHEST) / scale
    return (tracks, coverage, grad.astype(jnp.bfloat16), kernel_gradient)


def solution(mesh):
    return jax.shard_map(
        shards,
        mesh=mesh,
        in_specs=(
            P("seq", "chan"),
            P(None, None, None, "chan"),
            P(None, "chan"),
            P("seq", "chan"),
            P("seq", None),
        ),
        out_specs=(
            P("seq", "chan"),
            P("seq", "chan"),
            P("seq", "chan"),
            P(None, None, "seq", "chan"),
        ),
        check_vma=False,
    )
```

profile of v0, /device:TPU:2, one launch (start us, length us, event | category | flops | bytes accessed | tf_op | source)
XLA Modules:
  0.0 468.9 jit_solution(14514463337364591084)
XLA Ops:
  10.8 11.8 %collective-permute-done.1 = bf16[512,384]{1,0:T(8,128)(2,1)S(1)} collective-permute-done((bf16[512,384]{1,0:T(8,128)(2,1)}, bf16[512,384]{1,0:T(8,128)(2,1)S(1)}, u32[]{:S(2)}, u32[]{:S(2)}) %collective-permute-start.1) | collective-permute-done | bytes 393248 | tf_op jit(solution)/shard_map/ppermute | solution.py:13
  23.4 3.8 collective-permute-start
  27.3 8.0 %collective-permute-done = bf16[512,384]{1,0:T(8,128)(2,1)S(1)} collective-permute-done((bf16[512,384]{1,0:T(8,128)(2,1)}, bf16[512,384]{1,0:T(8,128)(2,1)S(1)}, u32[]{:S(2)}, u32[]{:S(2)}) %collective-permute-start) | collective-permute-done | bytes 393248 | tf_op jit(solution)/shard_map/ppermute | solution.py:13
  36.1 5.5 %all-gather.9.cloned.1.call-done = bf16[512,1536]{1,0:T(8,128)(2,1)} async-done(((bf16[512,384]{1,0:T(8,128)(2,1)}), bf16[512,1536]{1,0:T(8,128)(2,1)}) %all-gather.9.cloned.1.call-update) | async-done | bytes 1572880 | tf_op jit(solution)/shard_map/all_gather | solution.py:49
  41.5 3.6 fusion.10
  45.2 27.9 %all-gather.11.cloned.1.call-done = bf16[512,1536]{1,0:T(8,128)(2,1)} async-done(((bf16[512,384]{1,0:T(8,128)(2,1)}), bf16[512,1536]{1,0:T(8,128)(2,1)}) %all-gather.11.cloned.1.call-update) | async-done | bytes 1572880 | tf_op jit(solution)/shard_map/all_gather | solution.py:51
  73.1 3.6 fusion.6
  76.7 27.4 %all-gather.7.cloned.1.call-done = bf16[512,1536]{1,0:T(8,128)(2,1)} async-done(((bf16[512,384]{1,0:T(8,128)(2,1)}), bf16[512,1536]{1,0:T(8,128)(2,1)}) %all-gather.7.cloned.1.call-update) | async-done | bytes 1572880 | tf_op jit(solution)/shard_map/all_gather | solution.py:50
  104.1 3.9 fusion.3
  108.1 29.2 %all-gather.13.cloned.1.call-done = bf16[512,1536]{1,0:T(8,128)(2,1)} async-done(((bf16[512,384]{1,0:T(8,128)(2,1)}), bf16[512,1536]{1,0:T(8,128)(2,1)}) %all-gather.13.cloned.1.call-update) | async-done | bytes 1572880 | tf_op jit(solution)/shard_map/all_gather | solution.py:59
  137.4 5.8 %convert_reduce_fusion = (f32[4,1024]{1,0:T(4,128)}, bf16[512,1024]{1,0:T(8,128)(2,1)}, f32[512,1024]{1,0:T(8,128)S(1)}) fusion(bf16[512,1536]{1,0:T(8,128)(2,1)} %all-gather.13.cloned.1.call-done, bf16[1536,1024]{1,0:T(8,128)(2,1)S(1)} %copy-done), kind=kOutput, calls=%fused_computation.8 | convolution fusion | flops 1615327232 | bytes 7880704 | tf_op jit(solution)/shard_map/dot_general | solution.py:60
  143.2 3.5 fusion.15
  147.3 40.1 %reduce-scatter.4.cloned.1.call-done = f32[512,384]{1,0:T(8,128)} async-done(((f32[512,1536]{1,0:T(8,128)}), f32[512,384]{1,0:T(8,128)}) %reduce-scatter.4.cloned.1.call-update) | async-done | bytes 786448 | tf_op jit(solution)/shard_map/reduce_scatter | solution.py:63
  188.6 3.7 collective-permute-start.3
  196.0 4.8 %collective-permute-done.3 = bf16[512,384]{1,0:T(8,128)(2,1)S(1)} collective-permute-done((bf16[512,384]{1,0:T(8,128)(2,1)S(1)}, bf16[512,384]{1,0:T(8,128)(2,1)S(1)}, u32[]{:S(2)}, u32[]{:S(2)}) %collective-permute-start.3) | collective-permute-done | bytes 393248 | tf_op jit(solution)/shard_map/ppermute | solution.py:13
  201.8 3.1 collective-permute-done.2
  205.6 2.7 fusion
  208.6 2.6 convolution_bitcast_fusion.1
  213.3 3.3 pad_maximum_fusion
  217.4 50.6 %all-gather.15.cloned.1.call-done = f32[64,4,1024]{2,1,0:T(4,128)} async-done(((f32[1,4,1024]{2,1,0:T(4,128)}), f32[64,4,1024]{2,1,0:T(4,128)}) %all-gather.15.cloned.1.call-update) | async-done | bytes 1048592 | tf_op jit(solution)/shard_map/all_gather | solution.py:87
  268.0 2.6 reshape.20
  273.1 34.8 %reduce-scatter.6.cloned.1.call-done = f32[512,384]{1,0:T(8,128)} async-done(((f32[512,1536]{1,0:T(8,128)}), f32[512,384]{1,0:T(8,128)}) %reduce-scatter.6.cloned.1.call-update) | async-done | bytes 786448 | tf_op jit(solution)/shard_map/reduce_scatter | solution.py:75
  307.9 2.7 fusion.26
  310.6 151.5 %reduce-scatter.8.cloned.1.call-done = f32[3,24,384]{2,1,0:T(8,128)} async-done(((f32[3,1536,384]{2,1,0:T(8,128)}), f32[3,24,384]{2,1,0:T(8,128)}) %reduce-scatter.8.cloned.1.call-update) | async-done | bytes 110608 | tf_op jit(solution)/shard_map/reduce_scatter | solution.py:79
  (52 shorter events, 17.9 us)
Async XLA Ops:
  7.2 130.2 %copy-start = (bf16[1536,1024]{1,0:T(8,128)(2,1)S(1)}, bf16[1536,1024]{1,0:T(8,128)(2,1)}, u32[]{:S(2)}) copy-start(bf16[1536,1024]{1,0:T(8,128)(2,1)} %param.7) | copy-start | bytes 9437188
  7.2 34.4 %all-gather.9.cloned.1.call-start = ((), (), s32[]{:S(2)}) async-start(), calls=%async_computation.4 | async-start | bytes 1966080 | tf_op jit(solution)/shard_map/all_gather | solution.py:49
  9.4 63.7 %all-gather.11.cloned.1.call-start = ((), (), s32[]{:S(2)}) async-start(), calls=%async_computation.5 | async-start | bytes 1966080 | tf_op jit(solution)/shard_map/all_gather | solution.py:51
  9.5 13.1 %collective-permute-start.1 = (bf16[512,384]{1,0:T(8,128)(2,1)}, bf16[512,384]{1,0:T(8,128)(2,1)S(1)}, u32[]{:S(2)}, u32[]{:S(2)}) collective-permute-start(bf16[512,384]{1,0:T(8,128)(2,1)} %fusion.30), channel_id=1, source_target_pairs={{8,0},{12,4},{16,8},{20,12},{24,16},{28,20},{32,24},{36,28},{40,32... | collective-permute-start | bytes 1179656 | tf_op jit(solution)/shard_map/ppermute | solution.py:13
  22.6 0.7 copy-start.8
  23.4 80.7 %all-gather.7.cloned.1.call-start = ((), (), s32[]{:S(2)}) async-start(), calls=%async_computation.3 | async-start | bytes 1966080 | tf_op jit(solution)/shard_map/all_gather | solution.py:50
  23.4 11.8 %collective-permute-start = (bf16[512,384]{1,0:T(8,128)(2,1)}, bf16[512,384]{1,0:T(8,128)(2,1)S(1)}, u32[]{:S(2)}, u32[]{:S(2)}) collective-permute-start(bf16[512,384]{1,0:T(8,128)(2,1)} %fusion.30), channel_id=1, source_target_pairs={{0,8},{4,12},{8,16},{12,20},{16,24},{20,28},{24,32},{28,36},{32,40... | collective-permute-start | bytes 1179656 | tf_op jit(solution)/shard_map/ppermute | solution.py:13
  35.3 0.7 copy-start.9
  36.0 101.3 %all-gather.13.cloned.1.call-start = ((), (), s32[]{:S(2)}) async-start(), calls=%async_computation.6 | async-start | bytes 1966080 | tf_op jit(solution)/shard_map/all_gather | solution.py:59
  45.2 59.0 %copy-start.2 = (bf16[512,384]{1,0:T(8,128)(2,1)S(1)}, bf16[512,384]{1,0:T(8,128)(2,1)}, u32[]{:S(2)}) copy-start(bf16[512,384]{1,0:T(8,128)(2,1)} %param.5) | copy-start | bytes 1179652
  108.1 79.3 %reduce-scatter.4.cloned.1.call-start = ((), (), s32[]{:S(2)}) async-start(), calls=%async_computation.7 | async-start | bytes 3932160 | tf_op jit(solution)/shard_map/reduce_scatter | solution.py:63
  137.4 5.8 %copy-start.12 = (bf16[512,1024]{1,0:T(8,128)(2,1)S(1)}, bf16[512,1024]{1,0:T(8,128)(2,1)}, u32[]{:S(2)}) copy-start(bf16[512,1024]{1,0:T(8,128)(2,1)} %param.8) | copy-start | bytes 3145732
  146.7 121.3 %all-gather.15.cloned.1.call-start = ((), (), s32[]{:S(2)}) async-start(), calls=%async_computation.10 | async-start | bytes 1064960 | tf_op jit(solution)/shard_map/all_gather | solution.py:87
  147.3 160.6 %reduce-scatter.6.cloned.1.call-start = ((), (), s32[]{:S(2)}) async-start(), calls=%async_computation.8 | async-start | bytes 3932160 | tf_op jit(solution)/shard_map/reduce_scatter | solution.py:75
  188.6 7.4 %copy-start.3 = (bf16[512,384]{1,0:T(8,128)(2,1)}, bf16[512,384]{1,0:T(8,128)(2,1)S(1)}, u32[]{:S(2)}) copy-start(bf16[512,384]{1,0:T(8,128)(2,1)S(1)} %convert_element_type.37) | copy-start | bytes 1179652
  188.6 12.1 %copy-start.1 = (bf16[1,3,1536,384]{3,2,1,0:T(8,128)(2,1)S(1)}, bf16[1,3,1536,384]{3,2,1,0:T(8,128)(2,1)}, u32[]{:S(2)}) copy-start(bf16[1,3,1536,384]{3,2,1,0:T(8,128)(2,1)} %param.6) | copy-start | bytes 10616836
  188.6 12.1 %collective-permute-start.3 = (bf16[512,384]{1,0:T(8,128)(2,1)S(1)}, bf16[512,384]{1,0:T(8,128)(2,1)S(1)}, u32[]{:S(2)}, u32[]{:S(2)}) collective-permute-start(bf16[512,384]{1,0:T(8,128)(2,1)S(1)} %convert_element_type.37), channel_id=1, source_target_pairs={{0,8},{4,12},{8,16},{12,20},{16,24},{20,28},{24,32},{28,36},{32,40... | collective-permute-start | bytes 1179656 | tf_op jit(solution)/shard_map/ppermute | solution.py:13
  192.4 12.5 %collective-permute-start.2 = (bf16[512,384]{1,0:T(8,128)(2,1)S(1)}, bf16[512,384]{1,0:T(8,128)(2,1)S(1)}, u32[]{:S(2)}, u32[]{:S(2)}) collective-permute-start(bf16[512,384]{1,0:T(8,128)(2,1)S(1)} %convert_element_type.37), channel_id=1, source_target_pairs={{8,0},{12,4},{16,8},{20,12},{24,16},{28,20},{32,24},{36,28},{40,32... | collective-permute-start | bytes 1179656 | tf_op jit(solution)/shard_map/ppermute | solution.py:13
  200.8 1.0 copy-start.6
  204.9 0.7 copy-start.4
  208.4 253.7 %reduce-scatter.8.cloned.1.call-start = ((), (), s32[]{:S(2)}) async-start(), calls=%async_computation.9 | async-start | bytes 7188480 | tf_op jit(solution)/shard_map/reduce_scatter | solution.py:79
  208.6 2.7 copy-start.7
  208.6 2.6 copy-start.11
  211.3 1.0 copy-start.5
  (1 other events, 0.7 us)
Sparse Core Ops, SparseCore 0:
  10.4 31.0 all-gather.8
  44.0 29.1 all-gather.10
  75.0 29.1 all-gather.6
  108.2 29.1 all-gather.12
  146.8 40.5 reduce-scatter.3
  190.6 77.3 all-gather.14
  270.6 37.2 reduce-scatter.5
  312.7 149.2 reduce-scatter.7
where the time goes:
time: 469 us
  waiting for transfers between devices  395 us (84%)
  matrix products  33.6 us (7%)
  between operations  14.3 us (3%)
  starting transfers between devices  10.7 us (2%)
  other arithmetic  9.47 us (2%)
  local copies, waits for them, and re-layouts  5.52 us (1%)
    reduce_scatter x1, waiting for transfers between devices, shards(): lax.psum_scatter(kernel, 'seq', scatter_dimension=1, tiled=True)  151 us
    all_gather x1, waiting for transfers between devices, shards(): all_blocks = lax.all_gather(block_partial_sums, 'seq', axis=0, tiled=True)  50.6 us
    reduce_scatter x1, waiting for transfers between devices, shards(): lax.psum_scatter(times_t(head_term, head_weight), 'chan', scatter_dimensi...  40.1 us
    reduce_scatter x1, waiting for transfers between devices, shards(): lax.psum_scatter(partial_value, 'chan', scatter_dimension=1, tiled=True)  34.8 us
    all_gather x1, waiting for transfers between devices, shards(): full_state = lax.all_gather(state, 'chan', axis=1, tiled=True)  29.2 us
    all_gather x1, waiting for transfers between devices, shards(): whole_up = lax.all_gather(upper, 'chan', axis=1, tiled=True)  27.9 us
    ppermute x4, waiting for transfers between devices, shifted(): lax.ppermute(value, axis, [(source, source + steps) for source in range(l...  27.7 us
    all_gather x1, waiting for transfers between devices, shards(): whole_low = lax.all_gather(lower, 'chan', axis=1, tiled=True)  27.4 us
  transfers between devices with their start and end apart: 12, of which 12 were waited for; matrix products, arithmetic and copies ran while one was open for 6% of the time, Pallas kernels for 0%

commit v1 on v0

--- a/solution.py
+++ b/solution.py
@@ -5,6 +5,12 @@
 
 BLOCK = 128
 EXONS = 8
+
+
+def gather_from_all(x, axis, dim):
+    length = lax.axis_size(axis)
+    repeats = [length if d == dim else 1 for d in range(x.ndim)]
+    return lax.all_to_all(jnp.tile(x, repeats), axis, split_axis=dim, concat_axis=dim, tiled=True)
 
 
 def shifted(value, axis, steps):
@@ -56,7 +62,7 @@
     )
     saved = [(state, whole, steps)]
     state = (state.astype(jnp.float32) + mixed).astype(jnp.bfloat16)
-    full_state = lax.all_gather(state, "chan", axis=1, tiled=True)
+    full_state = gather_from_all(state, "chan", 1)
     logits = jnp.dot(full_state, head_weight, preferred_element_type=jnp.float32)
     tracks = jax.nn.softplus(logits).astype(jnp.bfloat16)
     head_term = (head_cot.astype(jnp.float32) * jax.nn.sigmoid(logits)).astype(jnp.bfloat16)

time: 469 us -> 465 us (level)
  waiting for transfers between devices: 395 us -> 365 us
  blocking collectives: 0 us -> 24.2 us
    all_gather x1 -> x0, waiting for transfers between devices: 29.2 us -> none  [shards(): full_state = lax.all_gather(state, 'chan', axis=1, tiled=True)]
    all_to_all x0 -> x1, blocking collectives: none -> 24.2 us  [gather_from_all(): lax.all_to_all(jnp.tile(x, repeats), axis, split_axis=dim, concat_axis=di...]
  transfers between devices with their start and end apart: 12 -> 11, of which waited for: 12 -> 11; matrix products, arithmetic and copies ran while one was open for 6% -> 6% of each run, Pallas kernels for 0% -> 0%
where the time goes in v1:
time: 465 us
  waiting for transfers between devices  365 us (78%)
  matrix products  32.8 us (7%)
  blocking collectives  24.2 us (5%)
  between operations  14.3 us (3%)
  starting transfers between devices  10.6 us (2%)
  other arithmetic  9.47 us (2%)
  local copies, waits for them, and re-layouts  8.27 us (2%)
    reduce_scatter x1, waiting for transfers between devices, shards(): lax.psum_scatter(kernel, 'seq', scatter_dimension=1, tiled=True)  151 us
    all_gather x1, waiting for transfers between devices, shards(): all_blocks = lax.all_gather(block_partial_sums, 'seq', axis=0, tiled=True)  50.6 us
    reduce_scatter x1, waiting for transfers between devices, shards(): lax.psum_scatter(times_t(head_term, head_weight), 'chan', scatter_dimensi...  39.4 us
    reduce_scatter x1, waiting for transfers between devices, shards(): lax.psum_scatter(partial_value, 'chan', scatter_dimension=1, tiled=True)  34.7 us
    all_gather x1, waiting for transfers between devices, shards(): whole_up = lax.all_gather(upper, 'chan', axis=1, tiled=True)  27.9 us
    ppermute x4, waiting for transfers between devices, shifted(): lax.ppermute(value, axis, [(source, source + steps) for source in range(l...  27.7 us
    all_gather x1, waiting for transfers between devices, shards(): whole_low = lax.all_gather(lower, 'chan', axis=1, tiled=True)  27.4 us
    all_to_all x1, blocking collectives, gather_from_all(): lax.all_to_all(jnp.tile(x, repeats), axis, split_axis=dim, concat_axis=di...  24.2 us
  transfers between devices with their start and end apart: 11, of which 11 were waited for; matrix products, arithmetic and copies ran while one was open for 6% of the time, Pallas kernels for 0%

profile of v1, /device:TPU:2, one launch (start us, length us, event | category | flops | bytes accessed | tf_op | source)
XLA Modules:
  0.0 464.9 jit_solution(10573736296879879602)
XLA Ops:
  10.8 11.8 %collective-permute-done.1 = bf16[512,384]{1,0:T(8,128)(2,1)S(1)} collective-permute-done((bf16[512,384]{1,0:T(8,128)(2,1)}, bf16[512,384]{1,0:T(8,128)(2,1)S(1)}, u32[]{:S(2)}, u32[]{:S(2)}) %collective-permute-start.1) | collective-permute-done | bytes 393248 | tf_op jit(solution)/shard_map/ppermute | solution.py:19
  23.4 3.8 collective-permute-start
  27.3 8.0 %collective-permute-done = bf16[512,384]{1,0:T(8,128)(2,1)S(1)} collective-permute-done((bf16[512,384]{1,0:T(8,128)(2,1)}, bf16[512,384]{1,0:T(8,128)(2,1)S(1)}, u32[]{:S(2)}, u32[]{:S(2)}) %collective-permute-start) | collective-permute-done | bytes 393248 | tf_op jit(solution)/shard_map/ppermute | solution.py:19
  36.1 5.4 %all-gather.8.cloned.1.call-done = bf16[512,1536]{1,0:T(8,128)(2,1)} async-done(((bf16[512,384]{1,0:T(8,128)(2,1)}), bf16[512,1536]{1,0:T(8,128)(2,1)}) %all-gather.8.cloned.1.call-update) | async-done | bytes 1572880 | tf_op jit(solution)/shard_map/all_gather | solution.py:55
  41.5 3.6 fusion.10
  45.2 27.9 %all-gather.10.cloned.1.call-done = bf16[512,1536]{1,0:T(8,128)(2,1)} async-done(((bf16[512,384]{1,0:T(8,128)(2,1)}), bf16[512,1536]{1,0:T(8,128)(2,1)}) %all-gather.10.cloned.1.call-update) | async-done | bytes 1572880 | tf_op jit(solution)/shard_map/all_gather | solution.py:57
  73.1 3.6 fusion.6
  76.7 27.4 %all-gather.6.cloned.1.call-done = bf16[512,1536]{1,0:T(8,128)(2,1)} async-done(((bf16[512,384]{1,0:T(8,128)(2,1)}), bf16[512,1536]{1,0:T(8,128)(2,1)}) %all-gather.6.cloned.1.call-update) | async-done | bytes 1572880 | tf_op jit(solution)/shard_map/all_gather | solution.py:56
  104.1 3.2 fusion.3
  107.5 24.2 %all_to_all.9 = bf16[512,4,384]{2,0,1:T(8,128)(2,1)} all-to-all(bf16[512,4,384]{2,0,1:T(8,128)(2,1)S(1)} %tile.2), channel_id=1, replica_groups=mesh['seq'=64,'chan'=4] {'chan'}, dimensions={1} | all-to-all | bytes 3145728 | tf_op jit(solution)/shard_map/all_to_all | solution.py:13
  131.7 2.6 copy.10
  134.3 5.9 %convert_reduce_fusion = (f32[4,1024]{1,0:T(4,128)}, bf16[512,1024]{1,0:T(8,128)(2,1)}, f32[512,1024]{1,0:T(8,128)S(1)}) fusion(bf16[512,1536]{0,1:T(8,128)(2,1)} %bitcast.44, bf16[1536,1024]{1,0:T(8,128)(2,1)S(1)} %copy-done), kind=kOutput, calls=%fused_computation.8 | convolution fusion | flops 1615327232 | bytes 7880704 | tf_op jit(solution)/shard_map/dot_general | solution.py:66
  140.1 3.5 fusion.15
  144.3 39.4 %reduce-scatter.4.cloned.1.call-done = f32[512,384]{1,0:T(8,128)} async-done(((f32[512,1536]{1,0:T(8,128)}), f32[512,384]{1,0:T(8,128)}) %reduce-scatter.4.cloned.1.call-update) | async-done | bytes 786448 | tf_op jit(solution)/shard_map/reduce_scatter | solution.py:69
  184.9 3.8 collective-permute-start.3
  192.3 4.8 %collective-permute-done.3 = bf16[512,384]{1,0:T(8,128)(2,1)S(1)} collective-permute-done((bf16[512,384]{1,0:T(8,128)(2,1)S(1)}, bf16[512,384]{1,0:T(8,128)(2,1)S(1)}, u32[]{:S(2)}, u32[]{:S(2)}) %collective-permute-start.3) | collective-permute-done | bytes 393248 | tf_op jit(solution)/shard_map/ppermute | solution.py:19
  198.1 3.1 collective-permute-done.2
  201.9 2.7 fusion
  204.9 2.6 convolution_bitcast_fusion.1
  209.6 3.3 pad_maximum_fusion
  213.7 50.6 %all-gather.12.cloned.1.call-done = f32[64,4,1024]{2,1,0:T(4,128)} async-done(((f32[1,4,1024]{2,1,0:T(4,128)}), f32[64,4,1024]{2,1,0:T(4,128)}) %all-gather.12.cloned.1.call-update) | async-done | bytes 1048592 | tf_op jit(solution)/shard_map/all_gather | solution.py:93
  269.3 34.7 %reduce-scatter.6.cloned.1.call-done = f32[512,384]{1,0:T(8,128)} async-done(((f32[512,1536]{1,0:T(8,128)}), f32[512,384]{1,0:T(8,128)}) %reduce-scatter.6.cloned.1.call-update) | async-done | bytes 786448 | tf_op jit(solution)/shard_map/reduce_scatter | solution.py:81
  304.0 2.7 fusion.26
  306.7 151.3 %reduce-scatter.8.cloned.1.call-done = f32[3,24,384]{2,1,0:T(8,128)} async-done(((f32[3,1536,384]{2,1,0:T(8,128)}), f32[3,24,384]{2,1,0:T(8,128)}) %reduce-scatter.8.cloned.1.call-update) | async-done | bytes 110608 | tf_op jit(solution)/shard_map/reduce_scatter | solution.py:85
  (52 shorter events, 20.6 us)
Async XLA Ops:
  7.2 127.1 %copy-start = (bf16[1536,1024]{1,0:T(8,128)(2,1)S(1)}, bf16[1536,1024]{1,0:T(8,128)(2,1)}, u32[]{:S(2)}) copy-start(bf16[1536,1024]{1,0:T(8,128)(2,1)} %param.7) | copy-start | bytes 9437188
  7.2 34.4 %all-gather.8.cloned.1.call-start = ((), (), s32[]{:S(2)}) async-start(), calls=%async_computation.5 | async-start | bytes 1966080 | tf_op jit(solution)/shard_map/all_gather | solution.py:55
  9.4 63.7 %all-gather.10.cloned.1.call-start = ((), (), s32[]{:S(2)}) async-start(), calls=%async_computation.6 | async-start | bytes 1966080 | tf_op jit(solution)/shard_map/all_gather | solution.py:57
  9.5 13.1 %collective-permute-start.1 = (bf16[512,384]{1,0:T(8,128)(2,1)}, bf16[512,384]{1,0:T(8,128)(2,1)S(1)}, u32[]{:S(2)}, u32[]{:S(2)}) collective-permute-start(bf16[512,384]{1,0:T(8,128)(2,1)} %fusion.30), channel_id=1, source_target_pairs={{8,0},{12,4},{16,8},{20,12},{24,16},{28,20},{32,24},{36,28},{40,32... | collective-permute-start | bytes 1179656 | tf_op jit(solution)/shard_map/ppermute | solution.py:19
  22.6 0.7 copy-start.8
  23.4 80.7 %all-gather.6.cloned.1.call-start = ((), (), s32[]{:S(2)}) async-start(), calls=%async_computation.4 | async-start | bytes 1966080 | tf_op jit(solution)/shard_map/all_gather | solution.py:56
  23.4 11.8 %collective-permute-start = (bf16[512,384]{1,0:T(8,128)(2,1)}, bf16[512,384]{1,0:T(8,128)(2,1)S(1)}, u32[]{:S(2)}, u32[]{:S(2)}) collective-permute-start(bf16[512,384]{1,0:T(8,128)(2,1)} %fusion.30), channel_id=1, source_target_pairs={{0,8},{4,12},{8,16},{12,20},{16,24},{20,28},{24,32},{28,36},{32,40... | collective-permute-start | bytes 1179656 | tf_op jit(solution)/shard_map/ppermute | solution.py:19
  35.3 0.8 copy-start.9
  36.1 147.6 %reduce-scatter.4.cloned.1.call-start = ((), (), s32[]{:S(2)}) async-start(), calls=%async_computation.7 | async-start | bytes 3932160 | tf_op jit(solution)/shard_map/reduce_scatter | solution.py:69
  45.2 59.0 %copy-start.2 = (bf16[512,384]{1,0:T(8,128)(2,1)S(1)}, bf16[512,384]{1,0:T(8,128)(2,1)}, u32[]{:S(2)}) copy-start(bf16[512,384]{1,0:T(8,128)(2,1)} %param.5) | copy-start | bytes 1179652
  134.3 5.9 %copy-start.12 = (bf16[512,1024]{1,0:T(8,128)(2,1)S(1)}, bf16[512,1024]{1,0:T(8,128)(2,1)}, u32[]{:S(2)}) copy-start(bf16[512,1024]{1,0:T(8,128)(2,1)} %param.8) | copy-start | bytes 3145732
  143.6 120.7 %all-gather.12.cloned.1.call-start = ((), (), s32[]{:S(2)}) async-start(), calls=%async_computation.10 | async-start | bytes 1064960 | tf_op jit(solution)/shard_map/all_gather | solution.py:93
  144.2 159.8 %reduce-scatter.6.cloned.1.call-start = ((), (), s32[]{:S(2)}) async-start(), calls=%async_computation.8 | async-start | bytes 3932160 | tf_op jit(solution)/shard_map/reduce_scatter | solution.py:81
  184.9 7.4 %copy-start.3 = (bf16[512,384]{1,0:T(8,128)(2,1)}, bf16[512,384]{1,0:T(8,128)(2,1)S(1)}, u32[]{:S(2)}) copy-start(bf16[512,384]{1,0:T(8,128)(2,1)S(1)} %convert_element_type.37) | copy-start | bytes 1179652
  184.9 12.2 %copy-start.1 = (bf16[1,3,1536,384]{3,2,1,0:T(8,128)(2,1)S(1)}, bf16[1,3,1536,384]{3,2,1,0:T(8,128)(2,1)}, u32[]{:S(2)}) copy-start(bf16[1,3,1536,384]{3,2,1,0:T(8,128)(2,1)} %param.6) | copy-start | bytes 10616836
  184.9 12.1 %collective-permute-start.3 = (bf16[512,384]{1,0:T(8,128)(2,1)S(1)}, bf16[512,384]{1,0:T(8,128)(2,1)S(1)}, u32[]{:S(2)}, u32[]{:S(2)}) collective-permute-start(bf16[512,384]{1,0:T(8,128)(2,1)S(1)} %convert_element_type.37), channel_id=1, source_target_pairs={{0,8},{4,12},{8,16},{12,20},{16,24},{20,28},{24,32},{28,36},{32,40... | collective-permute-start | bytes 1179656 | tf_op jit(solution)/shard_map/ppermute | solution.py:19
  188.7 12.5 %collective-permute-start.2 = (bf16[512,384]{1,0:T(8,128)(2,1)S(1)}, bf16[512,384]{1,0:T(8,128)(2,1)S(1)}, u32[]{:S(2)}, u32[]{:S(2)}) collective-permute-start(bf16[512,384]{1,0:T(8,128)(2,1)S(1)} %convert_element_type.37), channel_id=1, source_target_pairs={{8,0},{12,4},{16,8},{20,12},{24,16},{28,20},{32,24},{36,28},{40,32... | collective-permute-start | bytes 1179656 | tf_op jit(solution)/shard_map/ppermute | solution.py:19
  197.0 1.0 copy-start.6
  201.2 0.7 copy-start.4
  204.7 253.3 %reduce-scatter.8.cloned.1.call-start = ((), (), s32[]{:S(2)}) async-start(), calls=%async_computation.9 | async-start | bytes 7188480 | tf_op jit(solution)/shard_map/reduce_scatter | solution.py:85
  204.9 2.7 copy-start.7
  204.9 2.6 copy-start.11
  207.6 1.0 copy-start.5
  212.9 0.7 copy-start.10
Sparse Core Ops, SparseCore 0:
  10.4 31.0 all-gather.7
  44.0 29.1 all-gather.9
  75.0 29.1 all-gather.5
  143.7 39.9 reduce-scatter.3
  186.9 77.3 all-gather.11
  266.7 37.2 reduce-scatter.5
  308.9 149.1 reduce-scatter.7
